TPU v7x, 512 devices: a whole 4x8x8 slice. The times are simulated.
512 devices in a mesh: row: 8 (over y), col: 4 (over x_lo, core), tm: 16 (over x_hi, z).
Axes of the slice: x: 4 (x_hi: 2, x_lo: 2; x = x_hi * 2 + x_lo), y: 8, z: 8, core: 2. Of those that a mesh axis runs over, the one named last changes fastest.
Arguments:
- filled_orbitals: bfloat16 [4, 1024, 1024], P('col', 'row', 'tm'), may hold values from -0.1875 to 0.1875
- empty_orbitals: bfloat16 [4, 1024, 3072], P('col', 'row', 'tm'), may hold values from -0.109375 to 0.109375
- filled_depth: bfloat16 [1024], P('tm'), may hold values from 0.019897461 to 2
- empty_depth: bfloat16 [3072], P('tm'), may hold values from 0.019897461 to 2
- time_points: float32 [16], P('tm'), may hold values from 0.05 to 8
- cosine_weights: float32 [16, 16], replicated, may hold values from -3 to 3
Outputs:
- polar_freq: float32 [16, 4, 1024, 4096], P(None, None, ('row', 'tm'), 'col')
All inputs are finite; a program needn't handle non-finite values.
Results may differ from a plain program's by a relative error of at most 0.0033.
Values may be sent and summed in bfloat16 or wider, within the bound.
A program may use at most 64 MiB of HBM per device.

v0:
```python
import jax
import jax.numpy as jnp
from jax import lax
from jax.sharding import PartitionSpec as P


def tile_product(left_points, right_points, depths, tau_value):
    band_count = left_points.shape[-1]
    weight_row = jnp.exp(-depths.reshape(-1).astype(jnp.float32) * tau_value)
    scaled = (
        right_points.reshape(-1, band_count).astype(jnp.float32) * weight_row[None, :]
    ).astype(jnp.bfloat16)
    return lax.dot_general(
        left_points.reshape(-1, band_count),
        scaled,
        (((1,), (1,)), ((), ())),
        preferred_element_type=jnp.float32,
    )


def on_device(
    filled_orbitals, empty_orbitals, filled_depth, empty_depth, time_points, cosine_weights
):
    tau_value = time_points[0]
    filled_rows, empty_rows = (
        lax.all_gather(filled_orbitals, "col", axis=0, tiled=True),
        lax.all_gather(empty_orbitals, "col", axis=0, tiled=True),
    )
    filled_columns, empty_columns = (
        lax.all_gather(filled_orbitals, "row", axis=1, tiled=True),
        lax.all_gather(empty_orbitals, "row", axis=1, tiled=True),
    )
    tile_width = filled_columns.shape[1]
    row_filled = lax.all_gather(filled_rows, "tm", axis=2, tiled=True)
    column_filled = lax.all_gather(filled_columns, "tm", axis=2, tiled=True)
    depth_filled = lax.all_gather(filled_depth.reshape(1, 1, -1), "tm", axis=2, tiled=True)
    row_empty = lax.all_gather(empty_rows, "tm", axis=2, tiled=True)
    column_empty = lax.all_gather(empty_columns, "tm", axis=2, tiled=True)
    depth_empty = lax.all_gather(empty_depth.reshape(1, 1, -1), "tm", axis=2, tiled=True)
    green_filled = tile_product(row_filled, column_filled, depth_filled, tau_value)
    green_empty = tile_product(row_empty, column_empty, depth_empty, tau_value)
    polar_time = (
        (-(green_filled * green_empty))
        .astype(jnp.bfloat16)
        .reshape(filled_rows.shape[0], filled_rows.shape[1], tile_width)
    )
    return jnp.einsum(
        "ft,tabc->fabc",
        cosine_weights,
        lax.all_to_all(polar_time[None], "tm", split_axis=2, concat_axis=0, tiled=True).astype(
            jnp.float32
        ),
        precision=lax.Precision.HIGHEST,
    )


def solution(mesh):
    in_specs = (P("col", "row", "tm"), P("col", "row", "tm"), P("tm"), P("tm"), P("tm"), P())
    out_specs = P(None, None, ("row", "tm"), "col")
    return jax.shard_map(
        on_device, mesh=mesh, in_specs=in_specs, out_specs=out_specs, check_vma=False
    )
```

profile of v0, /device:TPU:6, one launch (start us, length us, event | category | flops | bytes accessed | tf_op | source)
XLA Modules:
  0.0 462.7 jit_solution(9080968557008193648)
XLA Ops:
  6.5 5.6 %all_gather.33 = bf16[4,128,64]{1,2,0:T(8,128)(2,1)S(1)} all-gather(bf16[1,128,64]{1,2,0:T(8,128)(2,1)} %param.6), channel_id=1, replica_groups=mesh['row'=8,'col'=4,'tm'=16] {'col'}, dimensions={0}, use_global_device_ids=true | all-gather | bytes 81920 | tf_op jit(solution)/shard_map/all_gather | solution.py:26
  12.1 0.7 copy.12
  12.8 0.0 all-gather.7.cloned.1.call-start
  12.9 26.2 %all_gather.30 = bf16[1,1024,64]{1,2,0:T(8,128)(2,1)} all-gather(bf16[1,128,64]{1,2,0:T(8,128)(2,1)} %param.6), channel_id=1, replica_groups=mesh['row'=8,'col'=4,'tm'=16] {'row'}, dimensions={1}, use_global_device_ids=true | all-gather | bytes 147456 | tf_op jit(solution)/shard_map/all_gather | solution.py:30
  39.1 0.0 all-gather.13.cloned.1.call-start
  39.1 5.8 %all_gather.38 = bf16[4,128,192]{1,2,0:T(8,128)(2,1)S(1)} all-gather(bf16[1,128,192]{1,2,0:T(8,128)(2,1)} %param.7), channel_id=1, replica_groups=mesh['row'=8,'col'=4,'tm'=16] {'col'}, dimensions={0}, use_global_device_ids=true | all-gather | bytes 245760 | tf_op jit(solution)/shard_map/all_gather | solution.py:27
  45.0 0.8 copy.14
  45.8 0.0 all-gather.11.cloned.1.call-start
  45.9 25.3 %all_gather.35 = bf16[1,1024,192]{1,2,0:T(8,128)(2,1)} all-gather(bf16[1,128,192]{1,2,0:T(8,128)(2,1)} %param.7), channel_id=1, replica_groups=mesh['row'=8,'col'=4,'tm'=16] {'row'}, dimensions={1}, use_global_device_ids=true | all-gather | bytes 442368 | tf_op jit(solution)/shard_map/all_gather | solution.py:31
  71.8 1.3 dynamic-slice
  74.4 0.8 dynamic-update-slice
  75.2 0.8 dynamic-update-slice.1
  76.1 47.0 %all-reduce.2 = (bf16[1024]{0:T(1024)(128)(2,1)S(1)}, bf16[3072]{0:T(1024)(128)(2,1)S(1)}) all-reduce(bf16[1024]{0:T(1024)(128)(2,1)S(1)} %dynamic-update-slice, bf16[3072]{0:T(1024)(128)(2,1)S(1)} %dynamic-update-slice.1), channel_id=2, replica_groups=mesh['row'=8,'col'=4,'tm'=16] {'tm'}, use_global_device_ids=true, to_apply=%add | all-reduce | flops 4096 | bytes 16384
  123.1 1.6 copy.13
  124.7 67.3 %all-gather.7.cloned.1.call-done = bf16[1,1024,1024]{1,2,0:T(8,128)(2,1)} async-done(((bf16[1,1024,64]{1,2,0:T(8,128)(2,1)}), bf16[1,1024,1024]{1,2,0:T(8,128)(2,1)}) %all-gather.7.cloned.1.call-update) | async-done | bytes 2097168 | tf_op jit(solution)/shard_map/all_gather | solution.py:35
  192.0 4.3 fusion.5
  196.3 94.7 %all-gather.13.cloned.1.call-done = bf16[4,128,3072]{1,0,2:T(4,128)(2,1)} async-done(((bf16[4,128,192]{1,0,2:T(4,128)(2,1)}), bf16[4,128,3072]{1,0,2:T(4,128)(2,1)}) %all-gather.13.cloned.1.call-update) | async-done | bytes 3145744 | tf_op jit(solution)/shard_map/all_gather | solution.py:37
  291.0 4.3 copy.15
  295.3 116.9 %all-gather.11.cloned.1.call-done = bf16[1,1024,3072]{1,2,0:T(8,128)(2,1)} async-done(((bf16[1,1024,192]{1,2,0:T(8,128)(2,1)}), bf16[1,1024,3072]{1,2,0:T(8,128)(2,1)}) %all-gather.11.cloned.1.call-update) | async-done | bytes 6291472 | tf_op jit(solution)/shard_map/all_gather | solution.py:38
  412.2 7.0 %negate_convert_fusion = bf16[1024,512]{0,1:T(8,128)(2,1)S(1)} fusion(f32[1024,512]{0,1:T(8,128)} %fusion.5, bf16[512,3072]{1,0:T(8,128)(2,1)S(1)} %bitcast.34, bf16[1,1024,3072]{1,2,0:T(8,128)(2,1)} %all-gather.11.cloned.1.call-done, f32[3072]{0:T(1024)S(1)} %multiply_exponential_fusion), kind=kOutput, calls=%fused_computation.8 | convolution fusion | flops 3232235520 | bytes 12595200 | tf_op jit(solution)/shard_map/dot_general | solution.py:13
  419.2 0.8 copy.16
  420.0 32.1 %all_to_all.18 = bf16[1,4,128,1024]{3,1,0,2:T(4,128)(2,1)S(1)} all-to-all(bf16[1,4,128,1024]{3,1,0,2:T(4,128)(2,1)S(1)} %copy.16), channel_id=1, replica_groups=mesh['row'=8,'col'=4,'tm'=16] {'tm'}, dimensions={2} | all-to-all | bytes 2097152 | tf_op jit(solution)/shard_map/all_to_all | solution.py:50
  452.1 1.6 convolution_bitcast_fusion
  453.7 2.5 copy.19
  (12 shorter events, 0.1 us)
Async XLA Ops:
  6.5 445.5 %copy-start = (f32[16,16]{1,0:T(8,128)S(1)}, f32[16,16]{1,0:T(8,128)}, u32[]{:S(2)}) copy-start(f32[16,16]{1,0:T(8,128)} %param.11) | copy-start | bytes 3076
  6.5 116.6 %all-gather.9.cloned.1.call-start = ((), (), s32[]{:S(2)}) async-start(), calls=%async_computation.2 | async-start | bytes 1114112 | tf_op jit(solution)/shard_map/all_gather | solution.py:34
  12.8 179.2 %all-gather.7.cloned.1.call-start = ((), (), s32[]{:S(2)}) async-start(), calls=%async_computation.1 | async-start | bytes 2228224 | tf_op jit(solution)/shard_map/all_gather | solution.py:35
  39.1 251.9 %all-gather.13.cloned.1.call-start = ((), (), s32[]{:S(2)}) async-start(), calls=%async_computation.4 | async-start | bytes 3342336 | tf_op jit(solution)/shard_map/all_gather | solution.py:37
  45.8 366.4 %all-gather.11.cloned.1.call-start = ((), (), s32[]{:S(2)}) async-start(), calls=%async_computation.3 | async-start | bytes 6684672 | tf_op jit(solution)/shard_map/all_gather | solution.py:38
Sparse Core Ops, SparseCore 0:
  12.9 88.0 all-gather.8
  104.2 87.7 all-gather.6
  195.2 95.7 all-gather.12
  294.0 118.1 all-gather.10
where the time goes:
time: 464 us; the launch traced here: 463 us
  waiting for transfers between devices  279 us (60%)
  blocking collectives  142 us (31%)
  between operations  15.1 us (3%)
  local copies, waits for them, and re-layouts  13.8 us (3%)
  matrix products  12.9 us (3%)
    all_gather x1, waiting for transfers between devices, on_device(): column_empty = lax.all_gather(empty_columns, 'tm', axis=2, tiled=True)  117 us
    all_gather x1, waiting for transfers between devices, on_device(): row_empty = lax.all_gather(empty_rows, 'tm', axis=2, tiled=True)  94.7 us
    all_gather x1, waiting for transfers between devices, on_device(): column_filled = lax.all_gather(filled_columns, 'tm', axis=2, tiled=True)  67.3 us
    unnamed x1, blocking collectives  47 us
    all_to_all x1, blocking collectives, on_device(): lax.all_to_all(polar_time[None], 'tm', split_axis=2, concat_axis=0, tiled...  32.1 us
    all_gather x1, blocking collectives, on_device(): lax.all_gather(filled_orbitals, 'row', axis=1, tiled=True)  26.2 us
    all_gather x1, blocking collectives, on_device(): lax.all_gather(empty_orbitals, 'row', axis=1, tiled=True)  25.3 us
    dot_general x2, matrix products, tile_product(): lax.dot_general(left_points.reshape(-1, band_count), scaled, (((1,), (1,)...  11.3 us
  transfers between devices with their start and end apart: 4, of which 3 were waited for; matrix products, arithmetic and copies ran while one was open for 3% of the time, Pallas kernels for 0%

commit v1 on v0

v1 whole, which is shorter than its diff:
```python
import jax
import jax.numpy as jnp
from jax import lax
from jax.experimental import pallas as pl
from jax.experimental.pallas import tpu as pltpu
from jax.sharding import PartitionSpec as P

F32 = jnp.float32
BF16 = jnp.bfloat16
MESH = pl.DeviceIdType.MESH
NT_DIMS = (((1,), (1,)), ((), ()))

N_TM = 16
RING = 8
KHALF = 2048
KFILLED = 1024


def offset(i):
    return (1 - 2 * (i % 2)) * ((i + 1) // 2)


def gather_kernel(
    tp_ref, fo_ref, eo_ref, fd_ref, ed_ref, out_ref,
    msg, arrived, blocks, rowblk, dep, expo, scaled, left, ptile,
    s0_send, s0_recv, r_send, r_recv, s1_send, s1_recv, s2_send, s2_recv, p_send, p_recv,
):
    y = lax.axis_index("row")
    col = lax.axis_index("col")
    tm = lax.axis_index("tm")
    x_lo, core = col // 2, col % 2
    x_hi, z = tm // RING, tm % RING
    flip = (1 - x_lo) * 2 + core
    a = z + core * (y - z)
    b = y + core * (z - y)
    mine = x_hi * 4 + flip

    def at(ap, bp):
        return (bp + core * (ap - bp), col, x_hi * RING + ap + core * (bp - ap))

    def plus(v, d):
        return (v + d + 2 * RING) % RING

    a_right, a_left = at(plus(a, 1), b), at(plus(a, -1), b)
    b_right, b_left = at(a, plus(b, 1)), at(a, plus(b, -1))

    def row_device(e):
        q = e % 4
        return (y, (1 - q // 2) * 2 + q % 2, (e // 4) * RING + z)

    barrier = pltpu.get_barrier_semaphore()

    def greet(device):
        pl.semaphore_signal(barrier, inc=1, device_id=device, device_id_type=MESH)

    @pl.loop(0, N_TM)
    def _(t):
        greet((y, flip, t))

    for dev in (a_right, a_left, b_right, b_left):
        greet(dev)
    greet((y, col, (1 - x_hi) * RING + z))
    other = x_lo * 2 + 1 - core
    for xh in range(2):
        greet((y, other, xh * RING + z))
        greet((y, (1 - x_lo) * 2 + 1 - core, xh * RING + z))

    odd = tm % 2
    def arrange(f, e):
        tail = e[:, 128:192]
        low = jnp.concatenate([f, tail], axis=1)
        high = jnp.concatenate([tail, f], axis=1)
        return jnp.where(odd == 1, high, low), e[:, :128]

    f0, f1 = arrange(fo_ref[...].astype(F32), eo_ref[...].astype(F32))
    rows = jnp.concatenate([f0.reshape(N_TM, 8, 128), f1.reshape(N_TM, 8, 128)], axis=1)
    msg[:, 0:16, :] = rows.astype(BF16)
    d0, d1 = arrange(fd_ref[...].astype(F32), ed_ref[...].astype(F32))
    tau = jnp.full((1, 128), tp_ref[0], F32)
    t_hi = tau.astype(BF16).astype(F32)
    t_mid = (tau - t_hi).astype(BF16).astype(F32)
    t_low = tau - t_hi - t_mid
    aux = jnp.concatenate([d0, d1, t_hi, t_mid, t_low, jnp.zeros((11, 128), F32)], axis=0)
    msg[:, 16:32, :] = jnp.broadcast_to(aux.astype(BF16)[None], (N_TM, 16, 128))

    pl.semaphore_wait(barrier, 25)

    def s0_copy(to):
        return pltpu.make_async_remote_copy(
            src_ref=msg.at[to], dst_ref=arrived.at[tm], send_sem=s0_send.at[to],
            recv_sem=s0_recv.at[tm], device_id=(y, flip, to), device_id_type=MESH)

    @pl.loop(0, N_TM)
    def _(t):
        s0_copy((tm + t) % N_TM).start()

    def wait_recv(dst, sem, device):
        pltpu.make_async_remote_copy(
            src_ref=dst, dst_ref=dst, send_sem=sem, recv_sem=sem,
            device_id=device, device_id_type=MESH).wait_recv()

    def wait_send(src, sem, device):
        pltpu.make_async_remote_copy(
            src_ref=src, dst_ref=src, send_sem=sem, recv_sem=sem,
            device_id=device, device_id_type=MESH).wait_send()

    @pl.loop(0, N_TM)
    def _(t):
        wait_recv(arrived.at[t], s0_recv.at[t], b_right)

    lane = lax.broadcasted_iota(jnp.int32, (8, 128), 1)
    first = lane < 64
    for i in range(8):
        even = arrived[2 * i, 0:16, :].astype(F32)[0:8]
        oddb = arrived[2 * i + 1, 0:16, :].astype(F32)[0:8]
        fil = jnp.where(first, even, oddb)
        tail = jnp.where(first, oddb, even)
        m0 = arrived[i, 0:16, :].astype(F32)[8:16]
        m1 = arrived[8 + i, 0:16, :].astype(F32)[8:16]
        lo = jnp.concatenate([fil, m0], axis=0).astype(BF16)
        hi = jnp.concatenate([tail, m1], axis=0).astype(BF16)
        blocks[b, a, :, i * 128:(i + 1) * 128] = lo
        blocks[b, a, :, (8 + i) * 128:(9 + i) * 128] = hi
        rowblk[mine, :, i * 128:(i + 1) * 128] = lo
        rowblk[mine, :, (8 + i) * 128:(9 + i) * 128] = hi

    def s1_copy(i, rightward):
        ref = blocks.at[b, plus(a, offset(i))]
        k = (i + 1) // 2
        landed = 2 * (k + 1) - 1 if rightward else 2 * (k + 1)
        slot = 0 if rightward else 1
        return pltpu.make_async_remote_copy(
            src_ref=ref, dst_ref=ref, send_sem=s1_send.at[slot, k],
            recv_sem=s1_recv.at[landed], device_id=a_right if rightward else a_left,
            device_id_type=MESH)

    def s2_copy(k, i, way):
        bp = plus(b, -k if way == 0 else k)
        ref = blocks.at[bp, plus(a, offset(i))]
        return pltpu.make_async_remote_copy(
            src_ref=ref, dst_ref=ref, send_sem=s2_send.at[way, k, i],
            recv_sem=s2_recv.at[way, k, i], device_id=b_right if way == 0 else b_left,
            device_id_type=MESH)

    def row_copy(j):
        e = (mine + j) % 8
        return pltpu.make_async_remote_copy(
            src_ref=blocks.at[b, a], dst_ref=rowblk.at[mine], send_sem=r_send.at[e],
            recv_sem=r_recv.at[mine], device_id=row_device(e), device_id_type=MESH)

    s1_copy(0, True).start()
    s1_copy(0, False).start()
    s2_copy(0, 0, 0).start()
    s2_copy(0, 0, 1).start()

    @pl.loop(1, 8)
    def _(j):
        row_copy(j).start()

    for i in range(8):
        even = arrived[2 * i, 16:32, :].astype(F32)
        oddb = arrived[2 * i + 1, 16:32, :].astype(F32)
        m0 = arrived[i, 16:32, :].astype(F32)
        m1 = arrived[8 + i, 16:32, :].astype(F32)
        e0 = jnp.broadcast_to(even[0:1], (8, 128))
        o0 = jnp.broadcast_to(oddb[0:1], (8, 128))
        dep[:, i * 128:(i + 1) * 128] = jnp.where(first, e0, o0)
        dep[:, (8 + i) * 128:(9 + i) * 128] = jnp.where(first, o0, e0)
        dep[:, (16 + i) * 128:(17 + i) * 128] = jnp.broadcast_to(m0[1:2], (8, 128))
        dep[:, (24 + i) * 128:(25 + i) * 128] = jnp.broadcast_to(m1[1:2], (8, 128))

    @pl.loop(0, N_TM)
    def _(t):
        info = arrived[t, 16:32, :].astype(F32)
        tv = jnp.broadcast_to(info[2:3] + info[3:4] + info[4:5], (8, 128))
        for g in range(32):
            cut = slice(g * 128, (g + 1) * 128)
            expo[t, :, cut] = jnp.exp(-dep[:, cut] * tv)

    for i in range(1, 8):
        wait_recv(blocks.at[b, plus(a, offset(i))], s1_recv.at[i], a_left)
        if i in (1, 3, 5):
            s1_copy(i, True).start()
        elif i in (2, 4):
            s1_copy(i, False).start()
        s2_copy(0, i, 0).start()
        s2_copy(0, i, 1).start()

    def relay(k, n):
        for half in range(2):
            i = 2 * n + half

            def take(way):
                bp = plus(b, -k if way == 0 else k)
                wait_recv(blocks.at[bp, plus(a, offset(i))], s2_recv.at[way, k - 1, i], b_left)

            def hand(way):
                s2_copy(k, i, way).start()

            if k < 3:
                for way in range(2):
                    take(way)
                    hand(way)
            elif k == 3:
                take(0)
                pl.when(n < 2)(lambda: hand(0))
                take(1)
                pl.when(n >= 2)(lambda: hand(1))
            else:
                pl.when(n < 2)(lambda: take(0))
                pl.when(n >= 2)(lambda: take(1))

    def scale_rows(jj):
        e = (mine + jj) % 8

        @pl.when(jj > 0)
        def _():
            wait_recv(rowblk.at[e], r_recv.at[e], b_left)

        lo = rowblk[e].astype(F32)[0:8]
        hi = rowblk[e].astype(F32)[8:16]

        @pl.loop(0, N_TM // 2)
        def _(tp):
            at_row = pl.ds(pl.multiple_of(e * 128 + tp * 16, 16), 16)
            for part, src in ((0, lo), (1, hi)):
                cut = slice(part * KHALF, (part + 1) * KHALF)
                both = [src * expo[2 * tp + h, :, cut] for h in range(2)]
                scaled[at_row, cut] = jnp.concatenate(both, axis=0).astype(BF16)

    def load_left(slot, r):
        bp = plus(b, offset(r))

        @pl.loop(0, 4)
        def _(j):
            v = blocks[bp, pl.ds(2 * j, 2)].astype(F32)
            at_row = pl.ds(pl.multiple_of(slot * 64 + j * 16, 16), 16)
            left[at_row, 0:KHALF] = v[:, 0:8].reshape(16, KHALF).astype(BF16)
            left[at_row, KHALF:] = v[:, 8:16].reshape(16, KHALF).astype(BF16)

    def p_copy(d, r):
        return pltpu.make_async_remote_copy(
            src_ref=ptile.at[d, r], dst_ref=out_ref.at[x_hi, plus(b, offset(r))],
            send_sem=p_send.at[d, r], recv_sem=p_recv.at[x_hi, r],
            device_id=(y, flip, d * RING + z), device_id_type=MESH)

    def product(rs, n):
        m = 64 * len(rs)
        at_row = pl.ds(pl.multiple_of(n * 256, 256), 256)
        g_o = lax.dot_general(left[0:m, 0:KFILLED], scaled[at_row, 0:KFILLED], NT_DIMS,
                              preferred_element_type=F32)
        g_e = lax.dot_general(left[0:m, KFILLED:], scaled[at_row, KFILLED:], NT_DIMS,
                              preferred_element_type=F32)
        p = (-(g_o * g_e)).astype(BF16)
        d, q = n // 2, 2 * (n % 2)
        for s, r in enumerate(rs):
            for h in range(2):
                ptile[d, r, q + h] = p[s * 64:(s + 1) * 64, h * 128:(h + 1) * 128]

        @pl.when(n % 2 == 1)
        def _():
            for r in rs:
                p_copy(d, r).start()

    @pl.loop(0, 4)
    def _(n):
        relay(1, n)
        scale_rows(2 * n)
        scale_rows(2 * n + 1)

    for k, rs in ((2, (0, 1, 2)), (3, (3, 4)), (4, (5, 6)), (5, (7,))):
        for s, r in enumerate(rs):
            load_left(s, r)

        @pl.loop(0, 4)
        def _(n):
            if k < 5:
                relay(k, n)
            product(rs, n)

    for d in range(2):
        @pl.loop(0, 8)
        def _(r):
            wait_recv(out_ref.at[d, plus(b, offset(r))], p_recv.at[d, r], b_left)

    @pl.loop(0, N_TM)
    def _(t):
        wait_send(msg.at[t], s0_send.at[t], b_left)

    @pl.loop(1, 8)
    def _(j):
        wait_send(blocks.at[b, a], r_send.at[(mine + j) % 8], b_left)

    for slot, count in ((0, 4), (1, 3)):
        for k in range(count):
            wait_send(blocks.at[b, a], s1_send.at[slot, k], b_left)
    for way in range(2):
        for k in range(3):
            @pl.loop(0, 8)
            def _(i):
                wait_send(blocks.at[b, a], s2_send.at[way, k, i], b_left)

        @pl.loop(0, 4)
        def _(i):
            wait_send(blocks.at[b, a], s2_send.at[way, 3, 4 * way + i], b_left)

        @pl.loop(0, 8)
        def _(r):
            wait_send(ptile.at[way, r], p_send.at[way, r], b_left)


def gather_products(tp, fo, eo, fd, ed):
    vmem = pl.BlockSpec(memory_space=pltpu.VMEM)
    dma = pltpu.SemaphoreType.DMA
    return pl.pallas_call(
        gather_kernel,
        out_shape=jax.ShapeDtypeStruct((2, 8, 4, 64, 128), BF16),
        in_specs=[pl.BlockSpec(memory_space=pltpu.SMEM), vmem, vmem, vmem, vmem],
        out_specs=pl.BlockSpec(memory_space=pl.ANY),
        scratch_shapes=[
            pltpu.VMEM((16, 32, 128), BF16),
            pltpu.VMEM((16, 32, 128), BF16),
            pltpu.VMEM((8, 8, 16, KHALF), BF16),
            pltpu.VMEM((8, 16, KHALF), BF16),
            pltpu.VMEM((8, 2 * KHALF), F32),
            pltpu.VMEM((16, 8, 2 * KHALF), F32),
            pltpu.VMEM((1024, 2 * KHALF), BF16),
            pltpu.VMEM((192, 2 * KHALF), BF16),
            pltpu.VMEM((2, 8, 4, 64, 128), BF16),
            dma((16,)), dma((16,)), dma((8,)), dma((8,)), dma((2, 4)), dma((8,)),
            dma((2, 4, 8)), dma((2, 4, 8)), dma((2, 8)), dma((2, 8)),
        ],
        compiler_params=pltpu.CompilerParams(
            collective_id=0, has_side_effects=True, vmem_limit_bytes=40 * 1024 * 1024),
        cost_estimate=pl.CostEstimate(flops=2 * 1024 * 4096 * 512, bytes_accessed=2 ** 22,
                                      transcendentals=2 ** 16),
        name="gather_products",
    )(tp, fo, eo, fd, ed)


def transform_kernel(w_ref, p_ref, out_ref, kw, points):
    core = lax.axis_index("col") % 2

    @pl.when(pl.program_id(0) == 0)
    def _():
        rr = lax.broadcasted_iota(jnp.int32, (128, 16), 0)
        rc = lax.broadcasted_iota(jnp.int32, (128, 16), 1)
        up = jnp.where(rr // 8 == rc, 1.0, 0.0).astype(BF16)
        cr = lax.broadcasted_iota(jnp.int32, (16, 128), 0)
        cc = lax.broadcasted_iota(jnp.int32, (16, 128), 1)
        across = jnp.where(cc // 8 == cr, 1.0, 0.0).astype(BF16)
        r2 = lax.broadcasted_iota(jnp.int32, (128, 128), 0)
        c2 = lax.broadcasted_iota(jnp.int32, (128, 128), 1)
        keep = (r2 % 8) == (c2 % 8)
        rest = w_ref[...]
        for i in range(3):
            part = rest.astype(BF16)
            rest = rest - part.astype(F32)
            tall = jnp.dot(up, part, preferred_element_type=F32).astype(BF16)
            full = jnp.dot(tall, across, preferred_element_type=F32)
            kw[i] = jnp.where(keep, full, 0.0).astype(BF16)

    @pl.when(core == 0)
    def _():
        for n in range(2):
            for yp in range(8):
                points[(2 * yp + n) * 64:(2 * yp + n + 1) * 64, :] = p_ref[n, yp, 0]

    @pl.when(core == 1)
    def _():
        for n in range(2):
            v = p_ref[n, :, 0].astype(F32)
            for yp in range(8):
                piece = v[:, yp * 8:(yp + 1) * 8, :].reshape(64, 128)
                points[(2 * yp + n) * 64:(2 * yp + n + 1) * 64, :] = piece.astype(BF16)

    for c in range(4):
        pts = points[c * 256:(c + 1) * 256, :]
        total = lax.dot_general(kw[2], pts, NT_DIMS, preferred_element_type=F32)
        total += lax.dot_general(kw[1], pts, NT_DIMS, preferred_element_type=F32)
        total += lax.dot_general(kw[0], pts, NT_DIMS, preferred_element_type=F32)
        out_ref[:, 0, :, c * 256:(c + 1) * 256] = total.reshape(16, 8, 256)


def transform(w, p):
    return pl.pallas_call(
        transform_kernel,
        out_shape=jax.ShapeDtypeStruct((16, 4, 8, 1024), F32),
        grid=(4,),
        in_specs=[
            pl.BlockSpec((16, 16), lambda q: (0, 0)),
            pl.BlockSpec((2, 8, 1, 64, 128), lambda q: (0, 0, q, 0, 0)),
        ],
        out_specs=pl.BlockSpec((16, 1, 8, 1024), lambda q: (0, q, 0, 0)),
        scratch_shapes=[pltpu.VMEM((3, 128, 128), BF16), pltpu.VMEM((1024, 128), BF16)],
        compiler_params=pltpu.CompilerParams(vmem_limit_bytes=16 * 1024 * 1024),
        cost_estimate=pl.CostEstimate(flops=2 ** 28, bytes_accessed=3 * 2 ** 20, transcendentals=0),
        name="transform",
    )(w, p)


def on_device(
    filled_orbitals, empty_orbitals, filled_depth, empty_depth, time_points, cosine_weights
):
    p = gather_products(
        time_points,
        filled_orbitals.reshape(128, 64),
        empty_orbitals.reshape(128, 192),
        filled_depth.reshape(1, 64),
        empty_depth.reshape(1, 192),
    )
    return transform(cosine_weights, p)


def solution(mesh):
    in_specs = (P("col", "row", "tm"), P("col", "row", "tm"), P("tm"), P("tm"), P("tm"), P())
    out_specs = P(None, None, ("row", "tm"), "col")
    return jax.shard_map(
        on_device, mesh=mesh, in_specs=in_specs, out_specs=out_specs, check_vma=False
    )
```

time: 464 us -> 71.9 us (0.15)
  waiting for transfers between devices: 279 us -> 0 us
  blocking collectives: 142 us -> 0 us
  Pallas kernels: 0 us -> 67.3 us
  between operations: 15.1 us -> 0.69 us
  matrix products: 12.9 us -> 0 us
  local copies, waits for them, and re-layouts: 13.8 us -> 3.04 us
    all_gather x4 -> x0, waiting for transfers between devices: 279 us -> none  [the longest x1 117 us: on_device(): column_empty = lax.all_gather(empty_columns, 'tm', axis=2, tiled=True)]
    pallas_call x0 -> x2, Pallas kernels: none -> 67.3 us  [the longest x1 64.2 us: gather_products(): pl.pallas_call(gather_kernel, out_shape=jax.ShapeDtypeStruct((2, 8, 4, 64...]
    all_gather x4 -> x0, blocking collectives: 62.9 us -> none  [the longest x1 26.2 us: on_device(): lax.all_gather(filled_orbitals, 'row', axis=1, tiled=True)]
    unnamed x1 -> x0, blocking collectives: 47 us -> none
    all_to_all x1 -> x0, blocking collectives: 32.1 us -> none  [on_device(): lax.all_to_all(polar_time[None], 'tm', split_axis=2, concat_axis=0, tiled...]
    dot_general x3 -> x0, matrix products: 12.9 us -> none  [the longest x2 11.3 us: tile_product(): lax.dot_general(left_points.reshape(-1, band_count), scaled, (((1,), (1,)...]
    all_gather x4 -> x0, local copies, waits for them, and re-layouts: 7.45 us -> none  [the longest x1 4.31 us: on_device(): row_empty = lax.all_gather(empty_rows, 'tm', axis=2, tiled=True)]
  transfers between devices with their start and end apart: 4 -> 0, of which waited for: 3 -> 0; matrix products, arithmetic and copies ran while one was open for 3% -> 0% of each run, Pallas kernels for 0% -> 0%
where the time goes in v1:
time: 71.9 us; the launch traced here: 71.1 us
  Pallas kernels  67.3 us (94%)
  local copies, waits for them, and re-layouts  3.04 us (4%)
    pallas_call x1, Pallas kernels, gather_products(): pl.pallas_call(gather_kernel, out_shape=jax.ShapeDtypeStruct((2, 8, 4, 64...  64.2 us
    pallas_call x1, Pallas kernels, transform(): pl.pallas_call(transform_kernel, out_shape=jax.ShapeDtypeStruct((16, 4, 8...  3.17 us
    unnamed x6, local copies, waits for them, and re-layouts  2.38 us

profile of v1, /device:TPU:6, one launch (start us, length us, event | category | flops | bytes accessed | tf_op | source)
XLA Modules:
  0.0 71.1 jit_solution(18115033153126422658)
XLA Ops:
  0.7 0.7 reshape.15.ed_ref
  1.3 0.8 %copy.7 = bf16[1,128,64]{2,1,0:T(8,128)(2,1)S(1)} copy(bf16[1,128,64]{1,2,0:T(8,128)(2,1)} %param.6) | data formatting | bytes 32768 | tf_op args[0]
  2.1 0.9 %copy.8 = bf16[1,128,192]{2,1,0:T(8,128)(2,1)S(1)} copy(bf16[1,128,192]{1,2,0:T(8,128)(2,1)} %param.7) | data formatting | bytes 98304 | tf_op args[1]
  3.1 0.0 copy-start.1
  3.1 0.6 copy-done.1
  3.7 0.0 copy-start
  3.7 64.2 %gather_products.1.p_ref = bf16[2,8,4,64,128]{4,3,2,1,0:T(8,128)(2,1)S(1)} custom-call(f32[1]{0:T(128)S(6)} %copy.9.tp_ref, bf16[128,64]{1,0:T(8,128)(2,1)S(1)} %bitcast.4, bf16[128,192]{1,0:T(8,128)(2,1)S(1)} %bitcast.3, bf16[1,64]{1,0:T(2,128)(2,1)S(1)} %bitcast.5, bf16[1,192]{1,0:T(2,128)(2,1)S(1)} %reshape.15.ed_ref), custom_call_target="tpu_custom_call" | custom-call | flops 4294967296 | bytes 4194304 | tf_op jit(solution)/shard_map/gather_products/pallas_call | solution.py:315
  67.9 0.0 copy-done
  67.9 3.2 %transform.1 = f32[16,4,8,1024]{3,2,1,0:T(8,128)} custom-call(f32[16,16]{1,0:T(8,128)S(1)} %copy-done, bf16[2,8,4,64,128]{4,3,2,1,0:T(8,128)(2,1)S(1)} %gather_products.1.p_ref), custom_call_target="tpu_custom_call" | custom-call | flops 268435456 | bytes 3145728 | tf_op jit(solution)/shard_map/transform/pallas_call | solution.py:386
Async XLA Ops:
  3.1 0.7 copy-start.1
  3.7 64.2 %copy-start = (f32[16,16]{1,0:T(8,128)S(1)}, f32[16,16]{1,0:T(8,128)}, u32[]{:S(2)}) copy-start(f32[16,16]{1,0:T(8,128)} %w_ref.1) | copy-start | bytes 3076

commit v2 on v1

v2 whole, which is shorter than its diff:
```python
import jax
import jax.numpy as jnp
from jax import lax
from jax.experimental import pallas as pl
from jax.experimental.pallas import tpu as pltpu
from jax.sharding import PartitionSpec as P

F32 = jnp.float32
BF16 = jnp.bfloat16
MESH = pl.DeviceIdType.MESH
NT_DIMS = (((1,), (1,)), ((), ()))

N_TM = 16
RING = 8
KHALF = 2048
KFILLED = 1024


def offset(i):
    return (1 - 2 * (i % 2)) * ((i + 1) // 2)


def gather_kernel(
    tp_ref, fo_ref, eo_ref, fd_ref, ed_ref, out_ref,
    fo, eo, fd, ed, msg, arrived, info, infos, blocks, rowblk, dep, expo, scaled, left, ptile,
    in_sem, s0_send, s0_recv, i_send, i_recv, r_send, r_recv, s1_send, s1_recv,
    s2_send, s2_recv, p_send, p_recv,
):
    y = lax.axis_index("row")
    col = lax.axis_index("col")
    tm = lax.axis_index("tm")
    x_lo, core = col // 2, col % 2
    x_hi, z = tm // RING, tm % RING
    flip = (1 - x_lo) * 2 + core
    a = z + core * (y - z)
    b = y + core * (z - y)
    mine = x_hi * 4 + flip

    def at(ap, bp):
        return (bp + core * (ap - bp), col, x_hi * RING + ap + core * (bp - ap))

    def plus(v, d):
        return (v + d + 2 * RING) % RING

    b_right, b_left = at(a, plus(b, 1)), at(a, plus(b, -1))

    group = x_hi * 2 + x_lo
    sibling = (y, x_lo * 2 + 1 - core, tm)

    def row_index(g, c):
        return (g // 2) * 4 + (1 - g % 2) * 2 + c

    loads = [
        pltpu.make_async_copy(src, dst, in_sem.at[i])
        for i, (src, dst) in enumerate(((fo_ref, fo), (eo_ref, eo), (fd_ref, fd), (ed_ref, ed)))
    ]
    for load in loads:
        load.start()

    barrier = pltpu.get_barrier_semaphore()

    def greet(device):
        pl.semaphore_signal(barrier, inc=1, device_id=device, device_id_type=MESH)

    @pl.loop(0, N_TM)
    def _(t):
        greet((y, flip, t))

    greet((plus(y, 1), col, tm))
    greet((plus(y, -1), col, tm))

    @pl.when(core == 1)
    def _():
        for d in (2, -2):
            greet((plus(y, d), col, tm))

    greet(sibling)

    for load in loads:
        load.wait()

    odd = tm % 2

    def arrange(f, e, axis):
        tail = lax.slice_in_dim(e, 128, 192, axis=axis)
        low = jnp.concatenate([f, tail], axis=axis)
        high = jnp.concatenate([tail, f], axis=axis)
        return jnp.where(odd == 1, high, low), lax.slice_in_dim(e, 0, 128, axis=axis)

    f0, f1 = arrange(fo[...].astype(F32), eo[...].astype(F32), 0)
    rows = jnp.concatenate([f0.T.reshape(N_TM, 8, 128), f1.T.reshape(N_TM, 8, 128)], axis=1)
    msg[...] = rows.astype(BF16)

    pl.semaphore_wait(barrier, 19 + 2 * core)

    def s0_copy(to):
        return pltpu.make_async_remote_copy(
            src_ref=msg.at[to], dst_ref=arrived.at[tm], send_sem=s0_send.at[to],
            recv_sem=s0_recv.at[tm], device_id=(y, flip, to), device_id_type=MESH)

    def info_copy(to):
        return pltpu.make_async_remote_copy(
            src_ref=info, dst_ref=infos.at[tm], send_sem=i_send.at[to],
            recv_sem=i_recv.at[tm], device_id=(y, flip, to), device_id_type=MESH)

    @pl.loop(0, N_TM)
    def _(t):
        s0_copy((tm + t) % N_TM).start()

    d0, d1 = arrange(fd[...].astype(F32).reshape(1, 64), ed[...].astype(F32).reshape(1, 192), 1)
    tau = jnp.full((1, 128), tp_ref[0], F32)
    t_hi = tau.astype(BF16).astype(F32)
    t_mid = (tau - t_hi).astype(BF16).astype(F32)
    t_low = tau - t_hi - t_mid
    info[...] = jnp.concatenate(
        [d0, d1, t_hi, t_mid, t_low, jnp.zeros((11, 128), F32)], axis=0).astype(BF16)

    def wait_recv(dst, sem, device):
        pltpu.make_async_remote_copy(
            src_ref=dst, dst_ref=dst, send_sem=sem, recv_sem=sem,
            device_id=device, device_id_type=MESH).wait_recv()

    def wait_send(src, sem, device):
        pltpu.make_async_remote_copy(
            src_ref=src, dst_ref=src, send_sem=sem, recv_sem=sem,
            device_id=device, device_id_type=MESH).wait_send()

    @pl.loop(0, N_TM)
    def _(t):
        wait_recv(arrived.at[t], s0_recv.at[t], b_right)

    lane = lax.broadcasted_iota(jnp.int32, (8, 128), 1)
    first = lane < 64
    for i in range(8):
        even = arrived[2 * i].astype(F32)[0:8]
        oddb = arrived[2 * i + 1].astype(F32)[0:8]
        fil = jnp.where(first, even, oddb)
        tail = jnp.where(first, oddb, even)
        m0 = arrived[i].astype(F32)[8:16]
        m1 = arrived[8 + i].astype(F32)[8:16]
        lo = jnp.concatenate([fil, m0], axis=0).astype(BF16)
        hi = jnp.concatenate([tail, m1], axis=0).astype(BF16)
        blocks[b, a, :, i * 128:(i + 1) * 128] = lo
        blocks[b, a, :, (8 + i) * 128:(9 + i) * 128] = hi
        rowblk[mine, :, i * 128:(i + 1) * 128] = lo
        rowblk[mine, :, (8 + i) * 128:(9 + i) * 128] = hi

    def s1_copy(i, d, seen):
        ref = blocks.at[b, plus(a, offset(i))]
        return pltpu.make_async_remote_copy(
            src_ref=ref, dst_ref=ref, send_sem=s1_send.at[seen], recv_sem=s1_recv.at[seen],
            device_id=at(plus(a, d), b), device_id_type=MESH)

    def s2_copy(k, i, way):
        bp = plus(b, -k if way == 0 else k)
        ref = blocks.at[bp, plus(a, offset(i))]
        return pltpu.make_async_remote_copy(
            src_ref=ref, dst_ref=ref, send_sem=s2_send.at[way, k, i],
            recv_sem=s2_recv.at[way, k, i], device_id=b_right if way == 0 else b_left,
            device_id_type=MESH)

    def row_copy(j):
        g = (group + j) % 4
        return pltpu.make_async_remote_copy(
            src_ref=blocks.at[b, a], dst_ref=rowblk.at[mine], send_sem=r_send.at[j],
            recv_sem=r_recv.at[mine], device_id=(y, (g % 2) * 2 + core, (g // 2) * RING + z),
            device_id_type=MESH)

    def row_hand(j):
        ref = rowblk.at[row_index((group + j) % 4, core)]
        return pltpu.make_async_remote_copy(
            src_ref=ref, dst_ref=ref, send_sem=r_send.at[4 + j],
            recv_sem=r_recv.at[row_index((group + j) % 4, core)], device_id=sibling,
            device_id_type=MESH)

    s2_copy(0, 0, 0).start()
    s2_copy(0, 0, 1).start()
    for d, seen in ((1, 1), (-1, 2), (2, 3), (-2, 4)):
        s1_copy(0, d, seen).start()

    @pl.loop(1, 4)
    def _(j):
        row_copy(j).start()

    row_hand(0).start()

    @pl.loop(0, N_TM)
    def _(t):
        info_copy((tm + t) % N_TM).start()

    for i in range(1, 8):
        wait_recv(blocks.at[b, plus(a, offset(i))], s1_recv.at[i], b_left)
        if i == 3:
            s1_copy(3, 1, 5).start()
            s1_copy(3, 2, 7).start()
        elif i == 4:
            s1_copy(4, -1, 6).start()
        s2_copy(0, i, 0).start()
        s2_copy(0, i, 1).start()

    def relay(k, n):
        for half in range(2):
            i = 2 * n + half

            def take(way):
                bp = plus(b, -k if way == 0 else k)
                wait_recv(blocks.at[bp, plus(a, offset(i))], s2_recv.at[way, k - 1, i], b_left)

            def hand(way):
                s2_copy(k, i, way).start()

            if k < 3:
                for way in range(2):
                    take(way)
                    hand(way)
            elif k == 3:
                take(0)
                pl.when(n < 2)(lambda: hand(0))
                take(1)
                pl.when(n >= 2)(lambda: hand(1))
            else:
                pl.when(n < 2)(lambda: take(0))
                pl.when(n >= 2)(lambda: take(1))

    def scale_rows(e):
        lo = rowblk[e].astype(F32)[0:8]
        hi = rowblk[e].astype(F32)[8:16]

        @pl.loop(0, N_TM // 2)
        def _(tp):
            at_row = pl.ds(pl.multiple_of(e * 128 + tp * 16, 16), 16)
            for part, src in ((0, lo), (1, hi)):
                cut = slice(part * KHALF, (part + 1) * KHALF)
                both = [src * expo[2 * tp + h, :, cut] for h in range(2)]
                scaled[at_row, cut] = jnp.concatenate(both, axis=0).astype(BF16)

    def load_left(slot, r):
        bp = plus(b, offset(r))

        @pl.loop(0, 4)
        def _(j):
            v = blocks[bp, pl.ds(2 * j, 2)].astype(F32)
            at_row = pl.ds(pl.multiple_of(slot * 64 + j * 16, 16), 16)
            left[at_row, 0:KHALF] = v[:, 0:8].reshape(16, KHALF).astype(BF16)
            left[at_row, KHALF:] = v[:, 8:16].reshape(16, KHALF).astype(BF16)

    def p_copy(d, r):
        return pltpu.make_async_remote_copy(
            src_ref=ptile.at[d, r], dst_ref=out_ref.at[x_hi, plus(b, offset(r))],
            send_sem=p_send.at[d, r], recv_sem=p_recv.at[x_hi, r],
            device_id=(y, flip, d * RING + z), device_id_type=MESH)

    def product(rs, n):
        m = 64 * len(rs)
        at_row = pl.ds(pl.multiple_of(n * 256, 256), 256)
        g_o = lax.dot_general(scaled[at_row, 0:KFILLED], left[0:m, 0:KFILLED], NT_DIMS,
                              preferred_element_type=F32)
        g_e = lax.dot_general(scaled[at_row, KFILLED:], left[0:m, KFILLED:], NT_DIMS,
                              preferred_element_type=F32)
        p = (-(g_o * g_e)).T.astype(BF16)
        d, q = n // 2, 2 * (n % 2)
        for s, r in enumerate(rs):
            for h in range(2):
                ptile[d, r, q + h] = p[s * 64:(s + 1) * 64, h * 128:(h + 1) * 128]

        @pl.when(n % 2 == 1)
        def _():
            for r in rs:
                p_copy(d, r).start()

    relay(1, 0)

    @pl.loop(0, N_TM)
    def _(t):
        wait_recv(infos.at[t], i_recv.at[t], b_right)

    for i in range(8):
        even = infos[2 * i].astype(F32)
        oddb = infos[2 * i + 1].astype(F32)
        m0 = infos[i].astype(F32)
        m1 = infos[8 + i].astype(F32)
        e0 = jnp.broadcast_to(even[0:1], (8, 128))
        o0 = jnp.broadcast_to(oddb[0:1], (8, 128))
        dep[:, i * 128:(i + 1) * 128] = jnp.where(first, e0, o0)
        dep[:, (8 + i) * 128:(9 + i) * 128] = jnp.where(first, o0, e0)
        dep[:, (16 + i) * 128:(17 + i) * 128] = jnp.broadcast_to(m0[1:2], (8, 128))
        dep[:, (24 + i) * 128:(25 + i) * 128] = jnp.broadcast_to(m1[1:2], (8, 128))

    @pl.loop(0, N_TM)
    def _(t):
        v = infos[t].astype(F32)
        tv = jnp.broadcast_to(v[2:3] + v[3:4] + v[4:5], (8, 128))
        for g in range(32):
            cut = slice(g * 128, (g + 1) * 128)
            expo[t, :, cut] = jnp.exp(-dep[:, cut] * tv)

    @pl.loop(0, 4)
    def _(n):
        g = (group + n) % 4
        own, other = row_index(g, core), row_index(g, 1 - core)

        @pl.when(n > 0)
        def _():
            wait_recv(rowblk.at[own], r_recv.at[own], b_left)
            row_hand(n).start()

        scale_rows(own)
        wait_recv(rowblk.at[other], r_recv.at[other], b_left)
        scale_rows(other)
        pl.when(n < 3)(lambda: relay(1, n + 1))

    for k, rs in ((2, (0, 1, 2)), (3, (3, 4)), (4, (5, 6)), (5, (7,))):
        for s, r in enumerate(rs):
            load_left(s, r)

        @pl.loop(0, 4)
        def _(n):
            if k < 5:
                relay(k, n)
            product(rs, n)

    for d in range(2):
        @pl.loop(0, 8)
        def _(r):
            wait_recv(out_ref.at[d, plus(b, offset(r))], p_recv.at[d, r], b_left)

    @pl.loop(0, N_TM)
    def _(t):
        wait_send(msg.at[t], s0_send.at[t], b_left)
        wait_send(info, i_send.at[t], b_left)

    @pl.loop(1, 8)
    def _(j):
        wait_send(blocks.at[b, a], r_send.at[j], b_left)
        wait_send(blocks.at[b, a], s1_send.at[j], b_left)

    for way in range(2):
        for k in range(3):
            @pl.loop(0, 8)
            def _(i):
                wait_send(blocks.at[b, a], s2_send.at[way, k, i], b_left)

        @pl.loop(0, 4)
        def _(i):
            wait_send(blocks.at[b, a], s2_send.at[way, 3, 4 * way + i], b_left)

        @pl.loop(0, 8)
        def _(r):
            wait_send(ptile.at[way, r], p_send.at[way, r], b_left)


def gather_products(tp, fo, eo, fd, ed):
    hbm = pl.BlockSpec(memory_space=pltpu.HBM)
    dma = pltpu.SemaphoreType.DMA
    return pl.pallas_call(
        gather_kernel,
        out_shape=jax.ShapeDtypeStruct((2, 8, 4, 64, 128), BF16),
        in_specs=[pl.BlockSpec(memory_space=pltpu.SMEM), hbm, hbm, hbm, hbm],
        out_specs=pl.BlockSpec(memory_space=pl.ANY),
        scratch_shapes=[
            pltpu.VMEM(fo.shape, BF16), pltpu.VMEM(eo.shape, BF16),
            pltpu.VMEM(fd.shape, BF16), pltpu.VMEM(ed.shape, BF16),
            pltpu.VMEM((16, 16, 128), BF16), pltpu.VMEM((16, 16, 128), BF16),
            pltpu.VMEM((16, 128), BF16), pltpu.VMEM((16, 16, 128), BF16),
            pltpu.VMEM((8, 8, 16, KHALF), BF16),
            pltpu.VMEM((8, 16, KHALF), BF16),
            pltpu.VMEM((8, 2 * KHALF), F32),
            pltpu.VMEM((16, 8, 2 * KHALF), F32),
            pltpu.VMEM((1024, 2 * KHALF), BF16),
            pltpu.VMEM((192, 2 * KHALF), BF16),
            pltpu.VMEM((2, 8, 4, 64, 128), BF16),
            dma((4,)), dma((16,)), dma((16,)), dma((16,)), dma((16,)), dma((8,)), dma((8,)),
            dma((8,)), dma((8,)),
            dma((2, 4, 8)), dma((2, 4, 8)), dma((2, 8)), dma((2, 8)),
        ],
        compiler_params=pltpu.CompilerParams(
            collective_id=0, has_side_effects=True, vmem_limit_bytes=60 * 1024 * 1024),
        cost_estimate=pl.CostEstimate(flops=2 * 1024 * 4096 * 512, bytes_accessed=2 ** 22,
                                      transcendentals=2 ** 16),
        name="gather_products",
    )(tp, fo, eo, fd, ed)


def transform_kernel(w_ref, p_ref, out_ref, p, kw, points, result, p_sem, out_sem):
    core = lax.axis_index("col") % 2
    loads = [pltpu.make_async_copy(p_ref.at[:, :, q], p.at[q], p_sem.at[q]) for q in range(4)]
    for load in loads:
        load.start()

    rr = lax.broadcasted_iota(jnp.int32, (128, 16), 0)
    rc = lax.broadcasted_iota(jnp.int32, (128, 16), 1)
    up = jnp.where(rr // 8 == rc, 1.0, 0.0).astype(BF16)
    cr = lax.broadcasted_iota(jnp.int32, (16, 128), 0)
    cc = lax.broadcasted_iota(jnp.int32, (16, 128), 1)
    across = jnp.where(cc // 8 == cr, 1.0, 0.0).astype(BF16)
    r2 = lax.broadcasted_iota(jnp.int32, (128, 128), 0)
    c2 = lax.broadcasted_iota(jnp.int32, (128, 128), 1)
    keep = (r2 % 8) == (c2 % 8)
    rest = w_ref[...]
    for i in range(3):
        part = rest.astype(BF16)
        rest = rest - part.astype(F32)
        tall = jnp.dot(up, part, preferred_element_type=F32).astype(BF16)
        full = jnp.dot(tall, across, preferred_element_type=F32)
        kw[i * 128:(i + 1) * 128, :] = jnp.where(keep, full, 0.0).astype(BF16)

    stores = []
    for q in range(4):
        loads[q].wait()

        @pl.when(core == 0)
        def _():
            for n in range(2):
                for yp in range(8):
                    points[(2 * yp + n) * 64:(2 * yp + n + 1) * 64, :] = p[q, n, yp]

        @pl.when(core == 1)
        def _():
            for n in range(2):
                v = p[q, n].astype(F32)
                for yp in range(8):
                    piece = v[:, yp * 8:(yp + 1) * 8, :].reshape(64, 128)
                    points[(2 * yp + n) * 64:(2 * yp + n + 1) * 64, :] = piece.astype(BF16)

        for c in range(4):
            pts = points[c * 256:(c + 1) * 256, :]
            three = lax.dot_general(kw[...], pts, NT_DIMS, preferred_element_type=F32)
            total = three[256:384] + three[128:256] + three[0:128]
            result[:, q, :, c * 256:(c + 1) * 256] = total.reshape(16, 8, 256)
        store = pltpu.make_async_copy(result.at[:, q], out_ref.at[:, q], out_sem.at[q])
        store.start()
        stores.append(store)
    for store in stores:
        store.wait()


def transform(w, p):
    dma = pltpu.SemaphoreType.DMA
    return pl.pallas_call(
        transform_kernel,
        out_shape=jax.ShapeDtypeStruct((16, 4, 8, 1024), F32),
        in_specs=[pl.BlockSpec(memory_space=pltpu.VMEM), pl.BlockSpec(memory_space=pl.ANY)],
        out_specs=pl.BlockSpec(memory_space=pl.ANY),
        scratch_shapes=[
            pltpu.VMEM((4, 2, 8, 64, 128), BF16), pltpu.VMEM((384, 128), BF16),
            pltpu.VMEM((1024, 128), BF16), pltpu.VMEM((16, 4, 8, 1024), F32), dma((4,)), dma((4,)),
        ],
        compiler_params=pltpu.CompilerParams(vmem_limit_bytes=60 * 1024 * 1024),
        cost_estimate=pl.CostEstimate(flops=2 ** 28, bytes_accessed=3 * 2 ** 20, transcendentals=0),
        name="transform",
    )(w, p)


def on_device(
    filled_orbitals, empty_orbitals, filled_depth, empty_depth, time_points, cosine_weights
):
    p = gather_products(
        time_points,
        jnp.swapaxes(filled_orbitals, 1, 2).reshape(64, 128),
        jnp.swapaxes(empty_orbitals, 1, 2).reshape(192, 128),
        filled_depth,
        empty_depth,
    )
    return transform(cosine_weights, p)


def solution(mesh):
    in_specs = (P("col", "row", "tm"), P("col", "row", "tm"), P("tm"), P("tm"), P("tm"), P())
    out_specs = P(None, None, ("row", "tm"), "col")
    return jax.shard_map(
        on_device, mesh=mesh, in_specs=in_specs, out_specs=out_specs, check_vma=False
    )
```

time: 71.9 us -> 66.9 us (0.930)
  local copies, waits for them, and re-layouts: 3.04 us -> 0 us
  Pallas kernels: 67.3 us -> 65.5 us
    pallas_call x1, Pallas kernels: 64.2 us -> 61.4 us  [gather_products(): pl.pallas_call(gather_kernel, out_shape=jax.ShapeDtypeStruct((2, 8, 4, 64...]
    unnamed x6 -> x0, local copies, waits for them, and re-layouts: 2.38 us -> none
    pallas_call x1, Pallas kernels: 3.17 us -> 4.06 us  [transform(): pl.pallas_call(transform_kernel, out_shape=jax.ShapeDtypeStruct((16, 4, 8...]
where the time goes in v2:
time: 66.9 us; the launch traced here: 66.1 us
  Pallas kernels  65.5 us (98%)
    pallas_call x1, Pallas kernels, gather_products(): pl.pallas_call(gather_kernel, out_shape=jax.ShapeDtypeStruct((2, 8, 4, 64...  61.4 us
    pallas_call x1, Pallas kernels, transform(): pl.pallas_call(transform_kernel, out_shape=jax.ShapeDtypeStruct((16, 4, 8...  4.06 us

profile of v2, /device:TPU:6, one launch (start us, length us, event | category | flops | bytes accessed | tf_op | source)
XLA Modules:
  0.0 66.1 jit_solution(16586835080791999913)
XLA Ops:
  0.7 61.4 %gather_products.1.p_ref = bf16[2,8,4,64,128]{4,3,2,1,0:T(8,128)(2,1)} custom-call(f32[1]{0:T(128)S(6)} %copy.7.tp_ref, bf16[64,128]{1,0:T(8,128)(2,1)} %bitcast.7, bf16[192,128]{1,0:T(8,128)(2,1)} %bitcast.6, bf16[64]{0:T(256)(128)(2,1)} %fd_ref.1, bf16[192]{0:T(256)(128)(2,1)} %ed_ref.1), custom_call_target="tpu_custom_call" | custom-call | flops 4294967296 | bytes 4194304 | tf_op jit(solution)/shard_map/gather_products/pallas_call | solution.py:355
  62.1 4.1 %transform.1 = f32[16,4,8,1024]{3,2,1,0:T(8,128)} custom-call(f32[16,16]{1,0:T(8,128)} %w_ref.1, bf16[2,8,4,64,128]{4,3,2,1,0:T(8,128)(2,1)} %gather_products.1.p_ref), custom_call_target="tpu_custom_call" | custom-call | flops 268435456 | bytes 3145728 | tf_op jit(solution)/shard_map/transform/pallas_call | solution.py:439

commit v3 on v2

--- a/solution.py
+++ b/solution.py
@@ -62,9 +62,12 @@
     def greet(device):
         pl.semaphore_signal(barrier, inc=1, device_id=device, device_id_type=MESH)
 
-    @pl.loop(0, N_TM)
-    def _(t):
-        greet((y, flip, t))
+    def far(t):
+        return (t % 2) * RING + plus(z, 4 + offset(t // 2))
+
+    @pl.loop(0, N_TM)
+    def _(t):
+        greet((y, flip, far(t)))
 
     greet((plus(y, 1), col, tm))
     greet((plus(y, -1), col, tm))
@@ -105,7 +108,7 @@
 
     @pl.loop(0, N_TM)
     def _(t):
-        s0_copy((tm + t) % N_TM).start()
+        s0_copy(far(t)).start()
 
     d0, d1 = arrange(fd[...].astype(F32).reshape(1, 64), ed[...].astype(F32).reshape(1, 192), 1)
     tau = jnp.full((1, 128), tp_ref[0], F32)
@@ -186,7 +189,7 @@
 
     @pl.loop(0, N_TM)
     def _(t):
-        info_copy((tm + t) % N_TM).start()
+        info_copy(far(t)).start()
 
     for i in range(1, 8):
         wait_recv(blocks.at[b, plus(a, offset(i))], s1_recv.at[i], b_left)
@@ -244,10 +247,11 @@
             left[at_row, 0:KHALF] = v[:, 0:8].reshape(16, KHALF).astype(BF16)
             left[at_row, KHALF:] = v[:, 8:16].reshape(16, KHALF).astype(BF16)
 
-    def p_copy(d, r):
-        return pltpu.make_async_remote_copy(
-            src_ref=ptile.at[d, r], dst_ref=out_ref.at[x_hi, plus(b, offset(r))],
-            send_sem=p_send.at[d, r], recv_sem=p_recv.at[x_hi, r],
+    def p_copy(d, r, h):
+        two = pl.ds(2 * h, 2)
+        return pltpu.make_async_remote_copy(
+            src_ref=ptile.at[d, r, two], dst_ref=out_ref.at[x_hi, plus(b, offset(r)), two],
+            send_sem=p_send.at[d, r, h], recv_sem=p_recv.at[x_hi, r, h],
             device_id=(y, flip, d * RING + z), device_id_type=MESH)
 
     def product(rs, n):
@@ -263,10 +267,8 @@
             for h in range(2):
                 ptile[d, r, q + h] = p[s * 64:(s + 1) * 64, h * 128:(h + 1) * 128]
 
-        @pl.when(n % 2 == 1)
-        def _():
-            for r in rs:
-                p_copy(d, r).start()
+        for r in rs:
+            p_copy(d, r, n % 2).start()
 
     relay(1, 0)
 
@@ -322,7 +324,8 @@
     for d in range(2):
         @pl.loop(0, 8)
         def _(r):
-            wait_recv(out_ref.at[d, plus(b, offset(r))], p_recv.at[d, r], b_left)
+            for h in range(2):
+                wait_recv(out_ref.at[d, plus(b, offset(r)), 2 * h:2 * h + 2], p_recv.at[d, r, h], b_left)
 
     @pl.loop(0, N_TM)
     def _(t):
@@ -346,7 +349,8 @@
 
         @pl.loop(0, 8)
         def _(r):
-            wait_send(ptile.at[way, r], p_send.at[way, r], b_left)
+            for h in range(2):
+                wait_send(ptile.at[way, r, 2 * h:2 * h + 2], p_send.at[way, r, h], b_left)
 
 
 def gather_products(tp, fo, eo, fd, ed):
@@ -371,22 +375,18 @@
             pltpu.VMEM((2, 8, 4, 64, 128), BF16),
             dma((4,)), dma((16,)), dma((16,)), dma((16,)), dma((16,)), dma((8,)), dma((8,)),
             dma((8,)), dma((8,)),
-            dma((2, 4, 8)), dma((2, 4, 8)), dma((2, 8)), dma((2, 8)),
+            dma((2, 4, 8)), dma((2, 4, 8)), dma((2, 8, 2)), dma((2, 8, 2)),
         ],
         compiler_params=pltpu.CompilerParams(
-            collective_id=0, has_side_effects=True, vmem_limit_bytes=60 * 1024 * 1024),
+            collective_id=0, has_side_effects=True, vmem_limit_bytes=36 * 1024 * 1024),
         cost_estimate=pl.CostEstimate(flops=2 * 1024 * 4096 * 512, bytes_accessed=2 ** 22,
                                       transcendentals=2 ** 16),
         name="gather_products",
     )(tp, fo, eo, fd, ed)
 
 
-def transform_kernel(w_ref, p_ref, out_ref, p, kw, points, result, p_sem, out_sem):
+def transform_kernel(w_ref, p_ref, out_ref, kw, points, result, out_sem):
     core = lax.axis_index("col") % 2
-    loads = [pltpu.make_async_copy(p_ref.at[:, :, q], p.at[q], p_sem.at[q]) for q in range(4)]
-    for load in loads:
-        load.start()
-
     rr = lax.broadcasted_iota(jnp.int32, (128, 16), 0)
     rc = lax.broadcasted_iota(jnp.int32, (128, 16), 1)
     up = jnp.where(rr // 8 == rc, 1.0, 0.0).astype(BF16)
@@ -406,18 +406,16 @@
 
     stores = []
     for q in range(4):
-        loads[q].wait()
-
         @pl.when(core == 0)
         def _():
             for n in range(2):
                 for yp in range(8):
-                    points[(2 * yp + n) * 64:(2 * yp + n + 1) * 64, :] = p[q, n, yp]
+                    points[(2 * yp + n) * 64:(2 * yp + n + 1) * 64, :] = p_ref[n, yp, q]
 
         @pl.when(core == 1)
         def _():
             for n in range(2):
-                v = p[q, n].astype(F32)
+                v = p_ref[n, :, q].astype(F32)
                 for yp in range(8):
                     piece = v[:, yp * 8:(yp + 1) * 8, :].reshape(64, 128)
                     points[(2 * yp + n) * 64:(2 * yp + n + 1) * 64, :] = piece.astype(BF16)
@@ -439,13 +437,13 @@
     return pl.pallas_call(
         transform_kernel,
         out_shape=jax.ShapeDtypeStruct((16, 4, 8, 1024), F32),
-        in_specs=[pl.BlockSpec(memory_space=pltpu.VMEM), pl.BlockSpec(memory_space=pl.ANY)],
+        in_specs=[pl.BlockSpec(memory_space=pltpu.VMEM)] * 2,
         out_specs=pl.BlockSpec(memory_space=pl.ANY),
         scratch_shapes=[
-            pltpu.VMEM((4, 2, 8, 64, 128), BF16), pltpu.VMEM((384, 128), BF16),
-            pltpu.VMEM((1024, 128), BF16), pltpu.VMEM((16, 4, 8, 1024), F32), dma((4,)), dma((4,)),
+            pltpu.VMEM((384, 128), BF16), pltpu.VMEM((1024, 128), BF16),
+            pltpu.VMEM((16, 4, 8, 1024), F32), dma((4,)),
         ],
-        compiler_params=pltpu.CompilerParams(vmem_limit_bytes=60 * 1024 * 1024),
+        compiler_params=pltpu.CompilerParams(vmem_limit_bytes=36 * 1024 * 1024),
         cost_estimate=pl.CostEstimate(flops=2 ** 28, bytes_accessed=3 * 2 ** 20, transcendentals=0),
         name="transform",
     )(w, p)
@@ -454,12 +452,15 @@
 def on_device(
     filled_orbitals, empty_orbitals, filled_depth, empty_depth, time_points, cosine_weights
 ):
+    def hold(v):
+        return pltpu.with_memory_space_constraint(v, pltpu.HBM)
+
     p = gather_products(
         time_points,
-        jnp.swapaxes(filled_orbitals, 1, 2).reshape(64, 128),
-        jnp.swapaxes(empty_orbitals, 1, 2).reshape(192, 128),
-        filled_depth,
-        empty_depth,
+        hold(jnp.swapaxes(filled_orbitals, 1, 2).reshape(64, 128)),
+        hold(jnp.swapaxes(empty_orbitals, 1, 2).reshape(192, 128)),
+        hold(filled_depth),
+        hold(empty_depth),
     )
     return transform(cosine_weights, p)
 

time: 66.9 us -> 64.8 us (0.969)
  Pallas kernels: 65.5 us -> 63.9 us
    pallas_call x1, Pallas kernels: 4.06 us -> 2.6 us  [transform(): pl.pallas_call(transform_kernel, out_shape=jax.ShapeDtypeStruct((16, 4, 8...]
where the time goes in v3:
time: 64.8 us; the launch traced here: 64.5 us
  Pallas kernels  63.9 us (99%)
  between operations  0.68 us (1%)
    pallas_call x1, Pallas kernels, gather_products(): pl.pallas_call(gather_kernel, out_shape=jax.ShapeDtypeStruct((2, 8, 4, 64...  61.3 us
    pallas_call x1, Pallas kernels, transform(): pl.pallas_call(transform_kernel, out_shape=jax.ShapeDtypeStruct((16, 4, 8...  2.6 us

profile of v3, /device:TPU:6, one launch (start us, length us, event | category | flops | bytes accessed | tf_op | source)
XLA Modules:
  0.0 64.5 jit_solution(3562754598600817388)
XLA Ops:
  0.7 0.0 copy-start
  0.7 61.3 %gather_products.1.p_ref = bf16[2,8,4,64,128]{4,3,2,1,0:T(8,128)(2,1)S(1)} custom-call(f32[1]{0:T(128)S(6)} %copy.7.tp_ref, bf16[64,128]{1,0:T(8,128)(2,1)} %bitcast.7, bf16[192,128]{1,0:T(8,128)(2,1)} %bitcast.6, bf16[64]{0:T(256)(128)(2,1)} %fd_ref.1, bf16[192]{0:T(256)(128)(2,1)} %ed_ref.1), custom_call_target="tpu_custom_call" | custom-call | flops 4294967296 | bytes 4194304 | tf_op jit(solution)/shard_map/gather_products/pallas_call | solution.py:359
  61.9 0.0 copy-done
  61.9 2.6 %transform.1 = f32[16,4,8,1024]{3,2,1,0:T(8,128)} custom-call(f32[16,16]{1,0:T(8,128)S(1)} %copy-done, bf16[2,8,4,64,128]{4,3,2,1,0:T(8,128)(2,1)S(1)} %gather_products.1.p_ref), custom_call_target="tpu_custom_call" | custom-call | flops 268435456 | bytes 3145728 | tf_op jit(solution)/shard_map/transform/pallas_call | solution.py:437
Async XLA Ops:
  0.7 61.3 %copy-start = (f32[16,16]{1,0:T(8,128)S(1)}, f32[16,16]{1,0:T(8,128)}, u32[]{:S(2)}) copy-start(f32[16,16]{1,0:T(8,128)} %w_ref.1) | copy-start | bytes 3076

commit v4 on v3

--- a/solution.py
+++ b/solution.py
@@ -191,16 +191,6 @@
     def _(t):
         info_copy(far(t)).start()
 
-    for i in range(1, 8):
-        wait_recv(blocks.at[b, plus(a, offset(i))], s1_recv.at[i], b_left)
-        if i == 3:
-            s1_copy(3, 1, 5).start()
-            s1_copy(3, 2, 7).start()
-        elif i == 4:
-            s1_copy(4, -1, 6).start()
-        s2_copy(0, i, 0).start()
-        s2_copy(0, i, 1).start()
-
     def relay(k, n):
         for half in range(2):
             i = 2 * n + half
@@ -270,7 +260,18 @@
         for r in rs:
             p_copy(d, r, n % 2).start()
 
-    relay(1, 0)
+    for i in range(1, 8):
+        wait_recv(blocks.at[b, plus(a, offset(i))], s1_recv.at[i], b_left)
+        if i == 3:
+            s1_copy(3, 1, 5).start()
+            s1_copy(3, 2, 7).start()
+        elif i == 4:
+            s1_copy(4, -1, 6).start()
+        s2_copy(0, i, 0).start()
+        s2_copy(0, i, 1).start()
+        if i == 4:
+            relay(1, 0)
+
 
     @pl.loop(0, N_TM)
     def _(t):

time: 64.8 us -> 64 us (0.988)
  Pallas kernels: 63.9 us -> 63.1 us
    pallas_call x1, Pallas kernels: 61.3 us -> 60.5 us  [gather_products(): pl.pallas_call(gather_kernel, out_shape=jax.ShapeDtypeStruct((2, 8, 4, 64...]
where the time goes in v4:
time: 64 us; the launch traced here: 63.8 us
  Pallas kernels  63.1 us (99%)
  between operations  0.68 us (1%)
    pallas_call x1, Pallas kernels, gather_products(): pl.pallas_call(gather_kernel, out_shape=jax.ShapeDtypeStruct((2, 8, 4, 64...  60.5 us
    pallas_call x1, Pallas kernels, transform(): pl.pallas_call(transform_kernel, out_shape=jax.ShapeDtypeStruct((16, 4, 8...  2.6 us

profile of v4, /device:TPU:6, one launch (start us, length us, event | category | flops | bytes accessed | tf_op | source)
XLA Modules:
  0.0 63.8 jit_solution(11911388487120498129)
XLA Ops:
  0.7 0.0 copy-start
  0.7 60.5 %gather_products.1.p_ref = bf16[2,8,4,64,128]{4,3,2,1,0:T(8,128)(2,1)S(1)} custom-call(f32[1]{0:T(128)S(6)} %copy.7.tp_ref, bf16[64,128]{1,0:T(8,128)(2,1)} %bitcast.7, bf16[192,128]{1,0:T(8,128)(2,1)} %bitcast.6, bf16[64]{0:T(256)(128)(2,1)} %fd_ref.1, bf16[192]{0:T(256)(128)(2,1)} %ed_ref.1), custom_call_target="tpu_custom_call" | custom-call | flops 4294967296 | bytes 4194304 | tf_op jit(solution)/shard_map/gather_products/pallas_call | solution.py:360
  61.2 0.0 copy-done
  61.2 2.6 %transform.1 = f32[16,4,8,1024]{3,2,1,0:T(8,128)} custom-call(f32[16,16]{1,0:T(8,128)S(1)} %copy-done, bf16[2,8,4,64,128]{4,3,2,1,0:T(8,128)(2,1)S(1)} %gather_products.1.p_ref), custom_call_target="tpu_custom_call" | custom-call | flops 268435456 | bytes 3145728 | tf_op jit(solution)/shard_map/transform/pallas_call | solution.py:438
Async XLA Ops:
  0.7 60.6 %copy-start = (f32[16,16]{1,0:T(8,128)S(1)}, f32[16,16]{1,0:T(8,128)}, u32[]{:S(2)}) copy-start(f32[16,16]{1,0:T(8,128)} %w_ref.1) | copy-start | bytes 3076

commit v5 on v4

--- a/solution.py
+++ b/solution.py
@@ -178,7 +178,7 @@
 
     s2_copy(0, 0, 0).start()
     s2_copy(0, 0, 1).start()
-    for d, seen in ((1, 1), (-1, 2), (2, 3), (-2, 4)):
+    for d, seen in ((2, 3), (-2, 4), (1, 1), (-1, 2)):
         s1_copy(0, d, seen).start()
 
     @pl.loop(1, 4)

time: 64 us -> 63.5 us (level)
  no operation moved by 1% of the time
where the time goes in v5:
time: 63.5 us; the launch traced here: 63.3 us
  Pallas kernels  62.7 us (99%)
  between operations  0.68 us (1%)
    pallas_call x1, Pallas kernels, gather_products(): pl.pallas_call(gather_kernel, out_shape=jax.ShapeDtypeStruct((2, 8, 4, 64...  60.1 us
    pallas_call x1, Pallas kernels, transform(): pl.pallas_call(transform_kernel, out_shape=jax.ShapeDtypeStruct((16, 4, 8...  2.6 us

profile of v5, /device:TPU:6, one launch (start us, length us, event | category | flops | bytes accessed | tf_op | source)
XLA Modules:
  0.0 63.3 jit_solution(10032437449402566187)
XLA Ops:
  0.7 0.0 copy-start
  0.7 60.1 %gather_products.1.p_ref = bf16[2,8,4,64,128]{4,3,2,1,0:T(8,128)(2,1)S(1)} custom-call(f32[1]{0:T(128)S(6)} %copy.7.tp_ref, bf16[64,128]{1,0:T(8,128)(2,1)} %bitcast.7, bf16[192,128]{1,0:T(8,128)(2,1)} %bitcast.6, bf16[64]{0:T(256)(128)(2,1)} %fd_ref.1, bf16[192]{0:T(256)(128)(2,1)} %ed_ref.1), custom_call_target="tpu_custom_call" | custom-call | flops 4294967296 | bytes 4194304 | tf_op jit(solution)/shard_map/gather_products/pallas_call | solution.py:360
  60.7 0.0 copy-done
  60.7 2.6 %transform.1 = f32[16,4,8,1024]{3,2,1,0:T(8,128)} custom-call(f32[16,16]{1,0:T(8,128)S(1)} %copy-done, bf16[2,8,4,64,128]{4,3,2,1,0:T(8,128)(2,1)S(1)} %gather_products.1.p_ref), custom_call_target="tpu_custom_call" | custom-call | flops 268435456 | bytes 3145728 | tf_op jit(solution)/shard_map/transform/pallas_call | solution.py:438
Async XLA Ops:
  0.7 60.1 %copy-start = (f32[16,16]{1,0:T(8,128)S(1)}, f32[16,16]{1,0:T(8,128)}, u32[]{:S(2)}) copy-start(f32[16,16]{1,0:T(8,128)} %w_ref.1) | copy-start | bytes 3076
